TPU v7x, 32 devices: a whole 2x2x4 slice. The times are simulated.
32 devices in a mesh: groups: 2 (over y), mesh: 8 (over z, x), sub: 2 (over core).
Axes of the slice: x: 2, y: 2, z: 4, core: 2. Of those that a mesh axis runs over, the one named last changes fastest.
Arguments:
- inputs: bfloat16 [65536, 227], P(('groups', 'mesh', 'sub')), parts along dimension 0, may hold values from -6 to 6
- targets: bfloat16 [65536, 227], P(('groups', 'mesh', 'sub')), parts along dimension 0, may hold values from -6 to 6
- node_weight: float32 [32768], P(('mesh', 'sub')), may hold values from 0.3 to 8, as said below
- w_embed: bfloat16 [227, 512], replicated, may hold values from -0.375 to 0.375
- w_mix: bfloat16 [512, 512], replicated, may hold values from -0.25 to 0.25
- w_back: bfloat16 [512, 512], replicated, may hold values from -0.25 to 0.25
- head_projection_weight: bfloat16 [512, 227], replicated, may hold values from -0.25 to 0.25
- enc_src: int32 [16, 5, 1024], P(('mesh', 'sub')), may hold values from 0 to 2047
- enc_dst: int32 [16, 5, 1024], P(('mesh', 'sub')), may hold values from 0 to 319
- enc_weight: float32 [16, 5, 1024], P(('mesh', 'sub')), may hold values from 0.25 to 1
- enc_count: int32 [16, 5], P(('mesh', 'sub')), may hold values from 256 to 1024, as said below
- proc_src: int32 [16, 2176], P(('mesh', 'sub')), may hold values from 0 to 5119, as said below
- proc_dst: int32 [16, 2176], P(('mesh', 'sub')), may hold values from 0 to 319
- proc_weight: float32 [16, 2176], P(('mesh', 'sub')), may hold values from 0.25 to 1
- proc_count: int32 [16], P(('mesh', 'sub')), may hold values from 1088 to 2176, as said below
- far_src: int32 [256, 4], P(('mesh', 'sub')), may hold values from 0 to 319
- far_dst: int32 [256, 4], P(('mesh', 'sub')), may hold values from 0 to 319
- far_weight: float32 [256, 4], P(('mesh', 'sub')), may hold values from -8 to 8
- far_count: int32 [256], P(('mesh', 'sub')), may hold values from 1 to 4, as said below
- dec_src: int32 [16, 5, 2048], P(('mesh', 'sub')), may hold values from 0 to 319
- dec_dst: int32 [16, 5, 2048], P(('mesh', 'sub')), may hold values from 0 to 2047
- dec_weight: float32 [16, 5, 2048], P(('mesh', 'sub')), may hold values from 0.25 to 1
- dec_count: int32 [16, 5], P(('mesh', 'sub')), may hold values from 512 to 2048, as said below
Outputs:
- prediction: bfloat16 [65536, 227], P(('groups', 'mesh', 'sub')), parts along dimension 0
- input_gradient: bfloat16 [65536, 227], P(('groups', 'mesh', 'sub')), parts along dimension 0
- embedding_weight_gradient: float32 [454, 512], P('groups'), parts along dimension 0
- mixing_weight_gradient: float32 [1024, 512], P('groups'), parts along dimension 0
- backward_weight_gradient: float32 [1024, 512], P('groups'), parts along dimension 0
- head_weight_gradient: float32 [1024, 227], P('groups'), parts along dimension 0
- loss: float32 [2], P('groups'), parts along dimension 0
There are 2 independent parts, one for each index of `groups`. A program takes and returns all parts, laid end to end along the dimension named above; an argument that names none is the same for every part. Nothing has to cross between parts.
Inputs may be any that keep to these rules, and one draw needn't show every extreme that they name: `enc_count`: in every draw all blocks whose partner is some one mesh shard have all 1024 slots live. `dec_count`: in every draw all blocks whose partner is some one mesh shard have all 2048 slots live. `proc_count`: some shard has all 2176 slots live in every draw. `proc_src`: row q holds mesh nodes q * 320 - 32 to (q + 1) * 320 + 31, taken modulo 5120. `far_count`: in every draw some destination shard has all 4 slots live from every owner. `node_weight`: positive weights.
All inputs are finite; a program needn't handle non-finite values.
Results may differ from a plain program's by a relative error of at most 0.013.
Values may be sent and summed in bfloat16 or wider, within the bound.
A program may use at most 192 MiB of HBM per device.

v0:
```python
import jax
import jax.numpy as jnp
from jax import lax
from jax.sharding import PartitionSpec as P

M_DEV = 320
REACH = 2
HALO = 32


EPS = 1e-05


def passed_along(block, axis, distance):
    devices = range(lax.axis_size(axis))
    route = [((i - distance) % len(devices), i) for i in devices]
    return lax.ppermute(block, axis, route)


def padded(shard, sides, width):
    for axis, dim in sides:
        count, length = (lax.axis_size(axis), shard.shape[dim])
        up = [(i, (i + 1) % count) for i in range(count)]
        down = [(j, i) for i, j in up]
        last = lax.slice_in_dim(shard, length - width, length, axis=dim)
        initial = lax.slice_in_dim(shard, 0, width, axis=dim)
        before = lax.ppermute(last, axis, up)
        after = lax.ppermute(initial, axis, down)
        shard = jnp.concatenate([before, shard, after], axis=dim)
    return shard


def norm_scale(values):
    return lax.rsqrt(jnp.mean(values * values, axis=-1, keepdims=True) + EPS)


def norm_back(upstream, normed_f, scale):
    return scale * (upstream - normed_f * jnp.mean(upstream * normed_f, axis=-1, keepdims=True))


def silu_slope(values):
    sigma = jax.nn.sigmoid(values)
    return sigma * (1.0 + values * (1.0 - sigma))


def slot_factor(weight, count):
    live_slot = lax.broadcasted_iota(jnp.int32, weight.shape, 1) < count[:, None]
    return jnp.where(live_slot, weight, 0.0)


def add_rows(factor, values, segment, total):
    columns = values.shape[-1]
    terms = factor.reshape(-1, 1) * values.reshape(-1, columns).astype(jnp.float32)
    return jax.ops.segment_sum(terms, segment.reshape(-1), num_segments=total)


def sum_rows(values, segment, total):
    columns = values.shape[-1]
    return jax.ops.segment_sum(
        values.reshape(-1, columns).astype(jnp.float32), segment.reshape(-1), num_segments=total
    )


def block_sum(terms, segment, total):
    return sum_rows(terms, segment, total).astype(jnp.bfloat16)


def push_blocks(terms, segment, total):
    summed = jnp.zeros((total, terms.shape[-1]), jnp.float32)
    for column in range(2 * REACH + 1):
        offset = column - REACH
        piece = terms[column]
        landing = segment[column]
        if offset != 0:
            piece, landing = passed_along((piece, landing), ("mesh", "sub"), offset)
        partial_value = block_sum(piece, landing, total)
        summed = summed + partial_value.astype(jnp.float32)
    return summed


def pull_blocks(values):
    pieces = []
    for column in range(2 * REACH + 1):
        offset = column - REACH
        if offset == 0:
            pieces.append(values)
        else:
            pieces.append(passed_along(values, ("mesh", "sub"), -offset))
    stacked = jnp.stack(pieces)
    return stacked.reshape(-1, values.shape[-1])


def send_far(values):
    return lax.all_to_all(values, ("mesh", "sub"), split_axis=0, concat_axis=0, tiled=True)


def contract_rows(left, right):
    return lax.dot_general(
        left, right, (((0,), (0,)), ((), ())), preferred_element_type=jnp.float32
    )


def times_transpose(left, right):
    return lax.dot_general(
        left, right, (((1,), (1,)), ((), ())), preferred_element_type=jnp.float32
    )


def per_device(
    inputs,
    targets,
    node_weight,
    w_embed,
    w_mix,
    w_back,
    head_projection_weight,
    enc_src,
    enc_dst,
    enc_weight,
    enc_count,
    proc_src,
    proc_dst,
    proc_weight,
    proc_count,
    far_src,
    far_dst,
    far_weight,
    far_count,
    dec_src,
    dec_dst,
    dec_weight,
    dec_count,
):
    shards = lax.axis_size(("mesh", "sub"))
    grid_rows = inputs.shape[0]
    mesh_rows = M_DEV
    total_grid = grid_rows * shards
    pre_embed = jnp.dot(inputs, w_embed, preferred_element_type=jnp.float32)
    embedded = jax.nn.silu(pre_embed).astype(jnp.bfloat16)
    enc_factor = slot_factor(enc_weight[0], enc_count[0])
    enc_message = (enc_factor[:, :, None] * embedded[enc_src[0]]).astype(jnp.bfloat16)
    gathered = push_blocks(enc_message, enc_dst[0], mesh_rows)
    mesh_scale = norm_scale(gathered)
    latent_f = gathered * mesh_scale
    mesh_latent = latent_f.astype(jnp.bfloat16)
    extended = padded(mesh_latent, ((("mesh", "sub"), 0),), HALO)
    first_node = lax.axis_index(("mesh", "sub")) * mesh_rows
    local_src = jnp.mod(proc_src[0] - first_node + HALO, mesh_rows * shards)
    proc_factor = slot_factor(proc_weight, proc_count)[0]
    far_factor = slot_factor(far_weight, far_count)
    far_rows = send_far(mesh_latent[far_src])
    proc_sum = add_rows(proc_factor, extended[local_src], proc_dst[0], mesh_rows) + add_rows(
        far_factor, far_rows, far_dst, mesh_rows
    )
    mixed_in = mesh_latent.astype(jnp.float32) + proc_sum
    proc_scale = norm_scale(mixed_in)
    proc_norm = mixed_in * proc_scale
    normed = proc_norm.astype(jnp.bfloat16)
    pre_mix = jnp.dot(normed, w_mix, preferred_element_type=jnp.float32)
    hidden = jax.nn.silu(pre_mix).astype(jnp.bfloat16)
    processed = (
        mesh_latent.astype(jnp.float32)
        + jnp.dot(hidden, w_back, preferred_element_type=jnp.float32)
    ).astype(jnp.bfloat16)
    near_processed = pull_blocks(processed)
    dec_index = lax.broadcasted_iota(jnp.int32, dec_src[0].shape, 0) * mesh_rows + dec_src[0]
    dec_factor = slot_factor(dec_weight[0], dec_count[0])
    dec_message = (dec_factor[:, :, None] * near_processed[dec_index]).astype(jnp.bfloat16)
    decoded = sum_rows(dec_message, dec_dst[0], grid_rows)
    grid_in = embedded.astype(jnp.float32) + decoded
    grid_scale = norm_scale(grid_in)
    grid_norm = grid_in * grid_scale
    grid_node_state = grid_norm.astype(jnp.bfloat16)
    predicted_fields = jnp.dot(
        grid_node_state, head_projection_weight, preferred_element_type=jnp.float32
    )
    residual_error = predicted_fields - targets.astype(jnp.float32)
    loss_part = 0.5 * jnp.sum(node_weight[:, None] * residual_error * residual_error)
    weighted_error = (node_weight[:, None] * residual_error).astype(jnp.bfloat16)
    d_state = times_transpose(weighted_error, head_projection_weight)
    d_grid = norm_back(d_state, grid_norm, grid_scale)
    dec_term = (dec_factor[:, :, None] * d_grid[dec_dst[0]]).astype(jnp.bfloat16)
    d_processed = push_blocks(dec_term, dec_src[0], mesh_rows)
    processed_grad = d_processed.astype(jnp.bfloat16)
    d_pre_mix = (times_transpose(processed_grad, w_back) * silu_slope(pre_mix)).astype(jnp.bfloat16)
    d_normed = times_transpose(d_pre_mix, w_mix)
    d_proc = norm_back(d_normed, proc_norm, proc_scale)
    spread = add_rows(proc_factor, d_proc[proc_dst[0]], local_src, mesh_rows + 2 * HALO)
    rims = jnp.concatenate([spread[:HALO], spread[mesh_rows + HALO :]], axis=0)
    returned = padded(rims, ((("mesh", "sub"), 0),), HALO)
    inner_part = spread[HALO : HALO + mesh_rows]
    from_left = jnp.pad(returned[:HALO], ((0, mesh_rows - HALO), (0, 0)))
    from_right = jnp.pad(returned[3 * HALO :], ((mesh_rows - HALO, 0), (0, 0)))
    far_term = (far_factor[:, :, None] * d_proc[far_dst]).astype(jnp.bfloat16)
    far_back = send_far(far_term)
    far_spread = sum_rows(far_back, far_src, mesh_rows)
    d_latent = d_processed + d_proc + inner_part + from_left + from_right + far_spread
    d_gathered = norm_back(d_latent, latent_f, mesh_scale)
    enc_back = d_gathered.astype(jnp.bfloat16)
    near_back = pull_blocks(enc_back)
    enc_index = lax.broadcasted_iota(jnp.int32, enc_dst[0].shape, 0) * mesh_rows + enc_dst[0]
    d_embedded = d_grid + add_rows(enc_factor, near_back[enc_index], enc_src[0], grid_rows)
    d_pre_embed = (d_embedded * silu_slope(pre_embed)).astype(jnp.bfloat16)
    input_gradient = times_transpose(d_pre_embed, w_embed).astype(jnp.bfloat16)
    totals = lax.psum(
        (
            contract_rows(inputs, d_pre_embed),
            contract_rows(normed, d_pre_mix),
            contract_rows(hidden, processed_grad),
            contract_rows(grid_node_state, weighted_error),
            loss_part.reshape(1),
        ),
        ("mesh", "sub"),
    )
    return (
        predicted_fields.astype(jnp.bfloat16),
        input_gradient,
        totals[0] / total_grid,
        totals[1] / total_grid,
        totals[2] / total_grid,
        totals[3] / total_grid,
        totals[4] / total_grid,
    )


def solution(mesh):
    placed = (
        P(("groups", "mesh", "sub"), None),
        P(("groups", "mesh", "sub"), None),
        P(("mesh", "sub")),
        P(),
        P(),
        P(),
        P(),
        P(("mesh", "sub"), None, None),
        P(("mesh", "sub"), None, None),
        P(("mesh", "sub"), None, None),
        P(("mesh", "sub"), None),
        P(("mesh", "sub"), None),
        P(("mesh", "sub"), None),
        P(("mesh", "sub"), None),
        P(("mesh", "sub")),
        P(("mesh", "sub"), None),
        P(("mesh", "sub"), None),
        P(("mesh", "sub"), None),
        P(("mesh", "sub")),
        P(("mesh", "sub"), None, None),
        P(("mesh", "sub"), None, None),
        P(("mesh", "sub"), None, None),
        P(("mesh", "sub"), None),
    )
    return jax.shard_map(
        per_device,
        mesh=mesh,
        in_specs=placed,
        out_specs=(
            P(("groups", "mesh", "sub"), None),
            P(("groups", "mesh", "sub"), None),
            P("groups", None),
            P("groups", None),
            P("groups", None),
            P("groups", None),
            P("groups"),
        ),
        check_vma=False,
    )
```

profile of v0, /device:TPU:0, one launch (start us, length us, event | category | flops | bytes accessed | tf_op | source)
XLA Modules:
  0.0 923.2 jit_solution(14126807723254047920)
XLA Ops:
  13.8 21.4 %gather_fusion = bf16[5120,512]{1,0:T(8,128)(2,1)} fusion(bf16[2048,512]{1,0:T(8,128)(2,1)S(1)} %get-tuple-element.18, s32[5120]{0:T(1024)S(1)} %broadcast_clamp_fusion.3), kind=kCustom, calls=%fused_computation | custom fusion | bytes 10506240 | tf_op jit(solution)/shard_map/gather | solution.py:141
  53.9 48.3 %collective-permute-done = s32[1024]{0:T(1024)S(1)} collective-permute-done((s32[1024]{0:T(1024)S(1)}, s32[1024]{0:T(1024)S(1)}, u32[]{:S(2)}, u32[]{:S(2)}) %collective-permute-start) | collective-permute-done | bytes 4128 | tf_op jit(solution)/shard_map/ppermute | solution.py:17
  104.9 8.5 collective-permute-start.4
  121.8 7.4 scatter_custom_fusion
  129.2 8.2 scatter_custom_fusion.1
  137.4 8.0 scatter_custom_fusion.3
  145.5 8.0 scatter_custom_fusion.4
  165.3 31.5 %scatter_custom_fusion.5 = f32[320,512]{1,0:T(8,128)} fusion(s32[2176]{0:T(1024)S(1)} %reduce, f32[2176]{0:T(1024)S(1)} %fusion.61, f32[]{:T(128)} %constant.24.clone.1, bf16[384,512]{1,0:T(8,128)(2,1)S(1)} %pad_maximum_fusion, s32[3072]{0:T(1024)S(1)} %pad_clamp_fusion.1), kind=kCustom, calls=%fused_computation.37 | custom fusion | flops 3342336 | bytes 1073156 | tf_op jit(solution)/shard_map/scatter-add | solution.py:54
  209.1 14.0 %collective-permute-done.10 = bf16[320,512]{1,0:T(8,128)(2,1)S(1)} collective-permute-done((bf16[320,512]{1,0:T(8,128)(2,1)S(1)}, bf16[320,512]{1,0:T(8,128)(2,1)S(1)}, u32[]{:S(2)}, u32[]{:S(2)}) %collective-permute-start.10) | collective-permute-done | bytes 327712 | tf_op jit(solution)/shard_map/ppermute | solution.py:17
  230.1 140.6 %scatter_custom_fusion.7 = f32[2048,512]{1,0:T(8,128)} fusion(f32[2048,512]{1,0:T(8,128)} %get-tuple-element.17, s32[10240]{0:T(1024)} %bitcast.123, f32[10240]{0:T(1024)S(1)} %copy-done.14, bf16[1600,512]{1,0:T(8,128)(2,1)} %bitcast.24, s32[10240]{0:T(1024)S(1)} %broadcast_clamp_fusion.1), kind=kCustom, calls=%fused_computation.27 | custom fusion | flops 26214400 | bytes 5914624 | tf_op jit(solution)/shard_map/scatter-add | solution.py:59
  381.4 45.5 %gather_fusion.2 = f32[10240,512]{1,0:T(8,128)} fusion(f32[2048,512]{1,0:T(8,128)} %subtract_multiply_fusion, s32[10240]{0:T(1024)S(1)} %broadcast_clamp_fusion), kind=kCustom, calls=%fused_computation.4 | custom fusion | bytes 41984000 | tf_op jit(solution)/shard_map/gather | solution.py:182
  426.9 8.1 multiply_convert_fusion
  448.4 66.7 %collective-permute-done.18 = s32[2048]{0:T(1024)S(1)} collective-permute-done((s32[2048]{0:T(1024)S(1)}, s32[2048]{0:T(1024)S(1)}, u32[]{:S(2)}, u32[]{:S(2)}) %collective-permute-start.18) | collective-permute-done | bytes 8224 | tf_op jit(solution)/shard_map/ppermute | solution.py:17
  515.0 65.8 %collective-permute-start.20 = (s32[2048]{0:T(1024)S(1)}, s32[2048]{0:T(1024)S(1)}, u32[]{:S(2)}, u32[]{:S(2)}) collective-permute-start(s32[2048]{0:T(1024)S(1)} %bitcast.128), channel_id=1, source_target_pairs={{14,0},{15,1},{0,2},{1,3},{2,4},{3,5},{4,6},{5,7},{6,8},{7,9},{8,1... | collective-permute-start | bytes 24584 | tf_op jit(solution)/shard_map/ppermute | solution.py:17
  591.1 13.5 %scatter_custom_fusion.10 = f32[320,512]{1,0:T(8,128)S(1)} fusion(s32[2048]{0:T(1024)S(1)} %bitcast.127, bf16[5,2048,512]{2,1,0:T(8,128)(2,1)} %copy-done.2, f32[]{:T(128)} %constant.24.clone.1), kind=kCustom, calls=%fused_computation.40 | custom fusion | flops 2097152 | bytes 2753024 | tf_op jit(solution)/shard_map/scatter-add | solution.py:59
  604.6 14.2 %scatter_custom_fusion.11 = f32[320,512]{1,0:T(8,128)} fusion(s32[2048]{0:T(1024)S(1)} %collective-permute-done.18, bf16[2048,512]{1,0:T(8,128)(2,1)} %collective-permute-done.19, f32[]{:T(128)} %constant.24.clone.1), kind=kCustom, calls=%fused_computation.45 | custom fusion | flops 2097152 | bytes 2752516 | tf_op jit(solution)/shard_map/scatter-add | solution.py:59
  618.8 14.1 %scatter_custom_fusion.12 = f32[320,512]{1,0:T(8,128)} fusion(s32[2048]{0:T(1024)S(1)} %collective-permute-done.20, bf16[2048,512]{1,0:T(8,128)(2,1)} %collective-permute-done.21, f32[]{:T(128)} %constant.24.clone.1), kind=kCustom, calls=%fused_computation.43 | custom fusion | flops 2097152 | bytes 2752516 | tf_op jit(solution)/shard_map/scatter-add | solution.py:59
  632.9 14.2 %scatter_custom_fusion.8 = f32[320,512]{1,0:T(8,128)} fusion(s32[2048]{0:T(1024)S(1)} %collective-permute-done.14, bf16[2048,512]{1,0:T(8,128)(2,1)} %collective-permute-done.15, f32[]{:T(128)} %constant.24.clone.1), kind=kCustom, calls=%fused_computation.49 | custom fusion | flops 2097152 | bytes 2752516 | tf_op jit(solution)/shard_map/scatter-add | solution.py:59
  647.1 14.4 %scatter_custom_fusion.9 = f32[320,512]{1,0:T(8,128)} fusion(s32[2048]{0:T(1024)S(1)} %collective-permute-done.16, bf16[2048,512]{1,0:T(8,128)(2,1)} %collective-permute-done.17, f32[]{:T(128)} %constant.24.clone.1), kind=kCustom, calls=%fused_computation.47 | custom fusion | flops 2097152 | bytes 2752516 | tf_op jit(solution)/shard_map/scatter-add | solution.py:59
  666.3 27.8 %scatter_custom_fusion.13 = f32[384,512]{1,0:T(8,128)} fusion(s32[2176]{0:T(1024)} %get-tuple-element.7, f32[2176]{0:T(1024)S(1)} %fusion.61, f32[]{:T(128)} %constant.24.clone.1, f32[320,512]{1,0:T(8,128)S(1)} %subtract_multiply_fusion.1, s32[3072]{0:T(1024)S(1)} %pad_clamp_fusion), kind=kCustom, calls=%fused_computation.35 | custom fusion | flops 2228224 | bytes 1463296 | tf_op jit(solution)/shard_map/scatter-add | solution.py:54
  730.6 9.0 collective-permute-done.27
  739.6 61.2 %scatter_custom_fusion.15 = f32[2048,512]{1,0:T(8,128)} fusion(f32[2048,512]{1,0:T(8,128)} %subtract_multiply_fusion, s32[5120]{0:T(1024)} %bitcast.124, f32[5120]{0:T(1024)S(1)} %copy-done.22, bf16[1600,512]{1,0:T(8,128)(2,1)S(1)} %bitcast.116, s32[5120]{0:T(1024)S(1)} %broadcast_clamp_fusion.2), kind=kCustom, calls=%fused_computation.32 | custom fusion | flops 7864320 | bytes 5873664 | tf_op jit(solution)/shard_map/scatter-add | solution.py:54
  807.9 31.1 %psum.39 = f32[1]{0:T(128)} all-reduce(f32[1]{0:T(128)} %bitcast.52), channel_id=1, replica_groups=mesh['groups'=2,'mesh'=8,'sub'=2] {'mesh','sub'}, use_global_device_ids=true, to_apply=%region_27.28 | all-reduce | flops 1 | bytes 8 | tf_op jit(solution)/shard_map/psum | solution.py:205
  841.4 67.1 %all-reduce.5.cloned.1.call-done = (f32[227,512]{1,0:T(8,128)}, f32[512,512]{1,0:T(8,128)}, f32[512,512]{1,0:T(8,128)}, f32[512,227]{0,1:T(8,128)}) async-done(((f32[227,512]{1,0:T(8,128)}, f32[512,512]{1,0:T(8,128)}, f32[512,512]{1,0:T(8,128)}, f32[512,227]{0,1:T(8,128)}), (f32[227,512]{1,0:T(8,128)}, f32[512,512]{1,0:T(8,128)}, f32[512,512]{1,0:T(8,128)}, ...) | async-done | bytes 3026960 | tf_op jit(solution)/shard_map/psum | solution.py:205
  (242 shorter events, 156.2 us)
Async XLA Ops:
  42.3 71.1 %collective-permute-start.1 = (bf16[1024,512]{1,0:T(8,128)(2,1)S(1)}, bf16[1024,512]{1,0:T(8,128)(2,1)S(1)}, u32[]{:S(2)}, u32[]{:S(2)}) collective-permute-start(bf16[1024,512]{1,0:T(8,128)(2,1)S(1)} %get-tuple-element.23), channel_id=1, source_target_pairs={{2,0},{3,1},{4,2},{5,3},{6,4},{7,5},{8,6},{9,7},{10,8},{11,9},{12,... | collective-permute-start | bytes 3145736 | tf_op jit(solution)/shard_map/ppermute | solution.py:17
  48.3 53.9 %collective-permute-start = (s32[1024]{0:T(1024)S(1)}, s32[1024]{0:T(1024)S(1)}, u32[]{:S(2)}, u32[]{:S(2)}) collective-permute-start(s32[1024]{0:T(1024)S(1)} %bitcast.134), channel_id=1, source_target_pairs={{2,0},{3,1},{4,2},{5,3},{6,4},{7,5},{8,6},{9,7},{10,8},{11,9},{12,... | collective-permute-start | bytes 12296 | tf_op jit(solution)/shard_map/ppermute | solution.py:17
  48.8 80.4 %collective-permute-start.3 = (bf16[1024,512]{1,0:T(8,128)(2,1)}, bf16[1024,512]{1,0:T(8,128)(2,1)}, u32[]{:S(2)}, u32[]{:S(2)}) collective-permute-start(bf16[1024,512]{1,0:T(8,128)(2,1)} %get-tuple-element.26), channel_id=1, source_target_pairs={{1,0},{2,1},{3,2},{4,3},{5,4},{6,5},{7,6},{8,7},{9,8},{10,9},{11,1... | collective-permute-start | bytes 3145736 | tf_op jit(solution)/shard_map/ppermute | solution.py:17
  49.1 88.4 %collective-permute-start.5 = (bf16[1024,512]{1,0:T(8,128)(2,1)}, bf16[1024,512]{1,0:T(8,128)(2,1)}, u32[]{:S(2)}, u32[]{:S(2)}) collective-permute-start(bf16[1024,512]{1,0:T(8,128)(2,1)} %get-tuple-element.25), channel_id=1, source_target_pairs={{15,0},{0,1},{1,2},{2,3},{3,4},{4,5},{5,6},{6,7},{7,8},{8,9},{9,10... | collective-permute-start | bytes 3145736 | tf_op jit(solution)/shard_map/ppermute | solution.py:17
  49.3 96.2 %collective-permute-start.7 = (bf16[1024,512]{1,0:T(8,128)(2,1)}, bf16[1024,512]{1,0:T(8,128)(2,1)}, u32[]{:S(2)}, u32[]{:S(2)}) collective-permute-start(bf16[1024,512]{1,0:T(8,128)(2,1)} %get-tuple-element.24), channel_id=1, source_target_pairs={{14,0},{15,1},{0,2},{1,3},{2,4},{3,5},{4,6},{5,7},{6,8},{7,9},{8,1... | collective-permute-start | bytes 3145736 | tf_op jit(solution)/shard_map/ppermute | solution.py:17
  104.9 32.5 %collective-permute-start.4 = (s32[1024]{0:T(1024)S(1)}, s32[1024]{0:T(1024)S(1)}, u32[]{:S(2)}, u32[]{:S(2)}) collective-permute-start(s32[1024]{0:T(1024)S(1)} %bitcast.131), channel_id=1, source_target_pairs={{15,0},{0,1},{1,2},{2,3},{3,4},{4,5},{5,6},{6,7},{7,8},{8,9},{9,10... | collective-permute-start | bytes 12296 | tf_op jit(solution)/shard_map/ppermute | solution.py:17
  113.4 32.1 %collective-permute-start.6 = (s32[1024]{0:T(1024)S(1)}, s32[1024]{0:T(1024)S(1)}, u32[]{:S(2)}, u32[]{:S(2)}) collective-permute-start(s32[1024]{0:T(1024)S(1)} %bitcast.130), channel_id=1, source_target_pairs={{14,0},{15,1},{0,2},{1,3},{2,4},{3,5},{4,6},{5,7},{6,8},{7,9},{8,1... | collective-permute-start | bytes 12296 | tf_op jit(solution)/shard_map/ppermute | solution.py:17
  161.3 35.5 %all-to-all-start = ((bf16[16,4,512]{2,1,0:T(4,128)(2,1)}), bf16[16,4,512]{2,1,0:T(4,128)(2,1)S(1)}, u32[]{:S(2)}, u32[]{:S(2)}) async-start(bf16[16,4,512]{2,1,0:T(4,128)(2,1)} %reshape.431), calls=%async_computation | async-start | bytes 131072 | tf_op jit(solution)/shard_map/all_to_all | solution.py:94
  202.5 20.6 %collective-permute-start.10 = (bf16[320,512]{1,0:T(8,128)(2,1)S(1)}, bf16[320,512]{1,0:T(8,128)(2,1)S(1)}, u32[]{:S(2)}, u32[]{:S(2)}) collective-permute-start(bf16[320,512]{1,0:T(8,128)(2,1)S(1)} %fusion.36), channel_id=1, source_target_pairs={{14,0},{15,1},{0,2},{1,3},{2,4},{3,5},{4,6},{5,7},{6,8},{7,9},{8,1... | collective-permute-start | bytes 983048 | tf_op jit(solution)/shard_map/ppermute | solution.py:17
  204.5 19.4 %collective-permute-start.11 = (bf16[320,512]{1,0:T(8,128)(2,1)S(1)}, bf16[320,512]{1,0:T(8,128)(2,1)S(1)}, u32[]{:S(2)}, u32[]{:S(2)}) collective-permute-start(bf16[320,512]{1,0:T(8,128)(2,1)S(1)} %fusion.36), channel_id=1, source_target_pairs={{15,0},{0,1},{1,2},{2,3},{3,4},{4,5},{5,6},{6,7},{7,8},{8,9},{9,10... | collective-permute-start | bytes 983048 | tf_op jit(solution)/shard_map/ppermute | solution.py:17
  204.5 20.9 %collective-permute-start.12 = (bf16[320,512]{1,0:T(8,128)(2,1)S(1)}, bf16[320,512]{1,0:T(8,128)(2,1)S(1)}, u32[]{:S(2)}, u32[]{:S(2)}) collective-permute-start(bf16[320,512]{1,0:T(8,128)(2,1)S(1)} %fusion.36), channel_id=1, source_target_pairs={{1,0},{2,1},{3,2},{4,3},{5,4},{6,5},{7,6},{8,7},{9,8},{10,9},{11,1... | collective-permute-start | bytes 983048 | tf_op jit(solution)/shard_map/ppermute | solution.py:17
  209.0 20.3 %collective-permute-start.13 = (bf16[320,512]{1,0:T(8,128)(2,1)S(1)}, bf16[320,512]{1,0:T(8,128)(2,1)S(1)}, u32[]{:S(2)}, u32[]{:S(2)}) collective-permute-start(bf16[320,512]{1,0:T(8,128)(2,1)S(1)} %fusion.36), channel_id=1, source_target_pairs={{2,0},{3,1},{4,2},{5,3},{6,4},{7,5},{8,6},{9,7},{10,8},{11,9},{12,... | collective-permute-start | bytes 983048 | tf_op jit(solution)/shard_map/ppermute | solution.py:17
  441.5 145.8 %collective-permute-start.19 = (bf16[2048,512]{1,0:T(8,128)(2,1)}, bf16[2048,512]{1,0:T(8,128)(2,1)}, u32[]{:S(2)}, u32[]{:S(2)}) collective-permute-start(bf16[2048,512]{1,0:T(8,128)(2,1)} %get-tuple-element.21), channel_id=1, source_target_pairs={{15,0},{0,1},{1,2},{2,3},{3,4},{4,5},{5,6},{6,7},{7,8},{8,9},{9,10... | collective-permute-start | bytes 6291464 | tf_op jit(solution)/shard_map/ppermute | solution.py:17
  441.5 177.3 %collective-permute-start.21 = (bf16[2048,512]{1,0:T(8,128)(2,1)}, bf16[2048,512]{1,0:T(8,128)(2,1)}, u32[]{:S(2)}, u32[]{:S(2)}) collective-permute-start(bf16[2048,512]{1,0:T(8,128)(2,1)} %get-tuple-element.20), channel_id=1, source_target_pairs={{14,0},{15,1},{0,2},{1,3},{2,4},{3,5},{4,6},{5,7},{6,8},{7,9},{8,1... | collective-permute-start | bytes 6291464 | tf_op jit(solution)/shard_map/ppermute | solution.py:17
  442.8 190.2 %collective-permute-start.15 = (bf16[2048,512]{1,0:T(8,128)(2,1)}, bf16[2048,512]{1,0:T(8,128)(2,1)}, u32[]{:S(2)}, u32[]{:S(2)}) collective-permute-start(bf16[2048,512]{1,0:T(8,128)(2,1)} %get-tuple-element.19), channel_id=1, source_target_pairs={{2,0},{3,1},{4,2},{5,3},{6,4},{7,5},{8,6},{9,7},{10,8},{11,9},{12,... | collective-permute-start | bytes 6291464 | tf_op jit(solution)/shard_map/ppermute | solution.py:17
  446.3 200.8 %collective-permute-start.17 = (bf16[2048,512]{1,0:T(8,128)(2,1)}, bf16[2048,512]{1,0:T(8,128)(2,1)}, u32[]{:S(2)}, u32[]{:S(2)}) collective-permute-start(bf16[2048,512]{1,0:T(8,128)(2,1)} %get-tuple-element.22), channel_id=1, source_target_pairs={{1,0},{2,1},{3,2},{4,3},{5,4},{6,5},{7,6},{8,7},{9,8},{10,9},{11,1... | collective-permute-start | bytes 6291464 | tf_op jit(solution)/shard_map/ppermute | solution.py:17
  447.4 67.6 %collective-permute-start.18 = (s32[2048]{0:T(1024)S(1)}, s32[2048]{0:T(1024)S(1)}, u32[]{:S(2)}, u32[]{:S(2)}) collective-permute-start(s32[2048]{0:T(1024)S(1)} %bitcast.129), channel_id=1, source_target_pairs={{15,0},{0,1},{1,2},{2,3},{3,4},{4,5},{5,6},{6,7},{7,8},{8,9},{9,10... | collective-permute-start | bytes 24584 | tf_op jit(solution)/shard_map/ppermute | solution.py:17
  515.0 70.2 %collective-permute-start.20 = (s32[2048]{0:T(1024)S(1)}, s32[2048]{0:T(1024)S(1)}, u32[]{:S(2)}, u32[]{:S(2)}) collective-permute-start(s32[2048]{0:T(1024)S(1)} %bitcast.128), channel_id=1, source_target_pairs={{14,0},{15,1},{0,2},{1,3},{2,4},{3,5},{4,6},{5,7},{6,8},{7,9},{8,1... | collective-permute-start | bytes 24584 | tf_op jit(solution)/shard_map/ppermute | solution.py:17
  585.3 47.7 %collective-permute-start.14 = (s32[2048]{0:T(1024)S(1)}, s32[2048]{0:T(1024)S(1)}, u32[]{:S(2)}, u32[]{:S(2)}) collective-permute-start(s32[2048]{0:T(1024)S(1)} %bitcast.126), channel_id=1, source_target_pairs={{2,0},{3,1},{4,2},{5,3},{6,4},{7,5},{8,6},{9,7},{10,8},{11,9},{12,... | collective-permute-start | bytes 24584 | tf_op jit(solution)/shard_map/ppermute | solution.py:17
  587.3 59.8 %collective-permute-start.16 = (s32[2048]{0:T(1024)S(1)}, s32[2048]{0:T(1024)S(1)}, u32[]{:S(2)}, u32[]{:S(2)}) collective-permute-start(s32[2048]{0:T(1024)S(1)} %bitcast.125), channel_id=1, source_target_pairs={{1,0},{2,1},{3,2},{4,3},{5,4},{6,5},{7,6},{8,7},{9,8},{10,9},{11,1... | collective-permute-start | bytes 24584 | tf_op jit(solution)/shard_map/ppermute | solution.py:17
  704.9 203.6 %all-reduce.5.cloned.1.call-start = ((), (), s32[]{:S(2)}) async-start(), calls=%async_computation.2 | async-start | bytes 6094848 | tf_op jit(solution)/shard_map/psum | solution.py:205
  713.6 13.5 %collective-permute-start.24 = (bf16[320,512]{1,0:T(8,128)(2,1)S(1)}, bf16[320,512]{1,0:T(8,128)(2,1)S(1)}, u32[]{:S(2)}, u32[]{:S(2)}) collective-permute-start(bf16[320,512]{1,0:T(8,128)(2,1)S(1)} %multiply_convert_fusion.5), channel_id=1, source_target_pairs={{14,0},{15,1},{0,2},{1,3},{2,4},{3,5},{4,6},{5,7},{6,8},{7,9},{8,1... | collective-permute-start | bytes 983048 | tf_op jit(solution)/shard_map/ppermute | solution.py:17
  716.5 12.6 %collective-permute-start.25 = (bf16[320,512]{1,0:T(8,128)(2,1)S(1)}, bf16[320,512]{1,0:T(8,128)(2,1)S(1)}, u32[]{:S(2)}, u32[]{:S(2)}) collective-permute-start(bf16[320,512]{1,0:T(8,128)(2,1)S(1)} %multiply_convert_fusion.5), channel_id=1, source_target_pairs={{15,0},{0,1},{1,2},{2,3},{3,4},{4,5},{5,6},{6,7},{7,8},{8,9},{9,10... | collective-permute-start | bytes 983048 | tf_op jit(solution)/shard_map/ppermute | solution.py:17
  722.5 17.1 %collective-permute-start.27 = (bf16[320,512]{1,0:T(8,128)(2,1)S(1)}, bf16[320,512]{1,0:T(8,128)(2,1)S(1)}, u32[]{:S(2)}, u32[]{:S(2)}) collective-permute-start(bf16[320,512]{1,0:T(8,128)(2,1)S(1)} %multiply_convert_fusion.5), channel_id=1, source_target_pairs={{2,0},{3,1},{4,2},{5,3},{6,4},{7,5},{8,6},{9,7},{10,8},{11,9},{12,... | collective-permute-start | bytes 983048 | tf_op jit(solution)/shard_map/ppermute | solution.py:17
  (51 other events, 1152.0 us)
Sparse Core Ops, SparseCore 0:
  807.4 101.1 all-reduce.4
where the time goes:
time: 933 us; the launch traced here: 923 us
  other arithmetic  414 us (44%)
  waiting for transfers between devices  224 us (24%)
  starting transfers between devices  122 us (13%)
  local copies, waits for them, and re-layouts  87.1 us (9%)
  blocking collectives  31.1 us (3%)
  matrix products  26.8 us (3%)
  between operations  18.5 us (2%)
    scatter-add x12, other arithmetic, sum_rows(): jax.ops.segment_sum(values.reshape(-1, columns).astype(jnp.float32), segm...  251 us
    ppermute x24, waiting for transfers between devices, passed_along(): return lax.ppermute(block, axis, route)  152 us
    scatter-add x4, other arithmetic, add_rows(): return jax.ops.segment_sum(terms, segment.reshape(-1), num_segments=total)  122 us
    ppermute x24, starting transfers between devices, passed_along(): return lax.ppermute(block, axis, route)  106 us
    psum x1, waiting for transfers between devices, per_device(): lax.psum((contract_rows(inputs, d_pre_embed), contract_rows(normed, d_pre...  67.1 us
    gather x1, local copies, waits for them, and re-layouts, per_device(): d_grid[dec_dst[0]]  45.5 us
    psum x1, blocking collectives, per_device(): lax.psum((contract_rows(inputs, d_pre_embed), contract_rows(normed, d_pre...  31.1 us
    gather x1, local copies, waits for them, and re-layouts, per_device(): embedded[enc_src[0]]  21.4 us
  transfers between devices with their start and end apart: 31, of which 12 were waited for; matrix products, arithmetic and copies ran while one was open for 15% of the time, Pallas kernels for 0%

commit v1 on v0

v1 whole, which is shorter than its diff:
```python
import jax
import jax.numpy as jnp
from jax import lax
from jax.sharding import PartitionSpec as P

M_DEV = 320
REACH = 2
HALO = 32


EPS = 1e-05


def passed_along(block, axis, distance):
    devices = range(lax.axis_size(axis))
    route = [((i - distance) % len(devices), i) for i in devices]
    return lax.ppermute(block, axis, route)


def norm_scale(values):
    return lax.rsqrt(jnp.mean(values * values, axis=-1, keepdims=True) + EPS)


def norm_back(upstream, normed_f, scale):
    return scale * (upstream - normed_f * jnp.mean(upstream * normed_f, axis=-1, keepdims=True))


def silu_slope(values):
    sigma = jax.nn.sigmoid(values)
    return sigma * (1.0 + values * (1.0 - sigma))


def slot_factor(weight, count):
    live_slot = lax.broadcasted_iota(jnp.int32, weight.shape, 1) < count[:, None]
    return jnp.where(live_slot, weight, 0.0)


def one_hot(index, total, factor=None):
    rows = lax.broadcasted_iota(jnp.int32, index.shape[:-1] + (total, index.shape[-1]), index.ndim - 1)
    hit = rows == index[..., None, :]
    marks = 1.0 if factor is None else factor[..., None, :]
    return jnp.where(hit, marks, 0.0).astype(jnp.bfloat16)


def edge_matrix(factor, to, to_total, start, start_total):
    left = one_hot(to, to_total, factor)
    right = one_hot(start, start_total)
    batch = tuple(range(to.ndim - 1))
    last = to.ndim
    return lax.dot_general(
        left, right, (((last,), (last,)), (batch, batch)), preferred_element_type=jnp.float32
    ).astype(jnp.bfloat16)


def push_blocks(partials, rows, beside):
    pieces = []
    for column in range(2 * REACH + 1):
        piece = partials[column * rows : (column + 1) * rows]
        offset = column - REACH
        if offset != 0:
            piece = passed_along(piece, ("mesh", "sub"), offset)
        pieces.append(piece)
    pieces, beside = lax.optimization_barrier((pieces, beside))
    summed = pieces[0].astype(jnp.float32)
    for piece in pieces[1:]:
        summed = summed + piece.astype(jnp.float32)
    return summed, beside


def pull_blocks(values):
    pieces = []
    for column in range(2 * REACH + 1):
        offset = column - REACH
        if offset == 0:
            pieces.append(values)
        else:
            pieces.append(passed_along(values, ("mesh", "sub"), -offset))
    return jnp.concatenate(pieces, axis=0)


def send_far(values):
    return lax.all_to_all(values, ("mesh", "sub"), split_axis=0, concat_axis=0, tiled=True)


def added_up(part, axes):
    shards = lax.axis_size(axes)
    count, width = part.shape
    share = -(-count // (16 * shards)) * 16
    part = jnp.pad(part, ((0, share * shards - count), (0, 0))).astype(jnp.bfloat16)
    shares = send_far(part.reshape(shards, share, width))
    total = jnp.sum(shares.astype(jnp.float32), axis=0).astype(jnp.bfloat16)
    spread = send_far(jnp.broadcast_to(total, (shards, share, width)))
    return spread.reshape(-1, width)[:count].astype(jnp.float32)


def contract_rows(left, right):
    return lax.dot_general(
        left, right, (((0,), (0,)), ((), ())), preferred_element_type=jnp.float32
    )


def times(left, right):
    return jnp.dot(left, right, preferred_element_type=jnp.float32)


def times_transpose(left, right):
    return lax.dot_general(
        left, right, (((1,), (1,)), ((), ())), preferred_element_type=jnp.float32
    )


def per_device(
    inputs,
    targets,
    node_weight,
    w_embed,
    w_mix,
    w_back,
    head_projection_weight,
    enc_src,
    enc_dst,
    enc_weight,
    enc_count,
    proc_src,
    proc_dst,
    proc_weight,
    proc_count,
    far_src,
    far_dst,
    far_weight,
    far_count,
    dec_src,
    dec_dst,
    dec_weight,
    dec_count,
):
    shards = lax.axis_size(("mesh", "sub"))
    grid_rows = inputs.shape[0]
    mesh_rows = M_DEV
    total_grid = grid_rows * shards
    pre_embed = jnp.dot(inputs, w_embed, preferred_element_type=jnp.float32)
    embedded = jax.nn.silu(pre_embed).astype(jnp.bfloat16)
    axes = ("mesh", "sub")
    enc_factor = slot_factor(enc_weight[0], enc_count[0])
    enc_matrix = edge_matrix(enc_factor, enc_dst[0], mesh_rows, enc_src[0], grid_rows)
    enc_matrix = enc_matrix.reshape(-1, grid_rows)
    dec_factor = slot_factor(dec_weight[0], dec_count[0])
    dec_matrix = edge_matrix(dec_factor, dec_src[0], mesh_rows, dec_dst[0], grid_rows)
    dec_matrix = dec_matrix.reshape(-1, grid_rows)
    first_node = lax.axis_index(axes) * mesh_rows
    local_src = jnp.mod(proc_src[0] - first_node + HALO, mesh_rows * shards)
    proc_factor = slot_factor(proc_weight, proc_count)[0]
    proc_matrix = edge_matrix(proc_factor, proc_dst[0], mesh_rows, local_src, mesh_rows + 2 * HALO)
    far_factor = slot_factor(far_weight, far_count).reshape(-1)
    far_into = one_hot(far_dst.reshape(-1), mesh_rows, far_factor)
    far_from = one_hot(far_src.reshape(-1), mesh_rows)
    enc_partial = times(enc_matrix, embedded).astype(jnp.bfloat16)
    gathered, (dec_matrix, proc_matrix, far_into, far_from) = push_blocks(
        enc_partial, mesh_rows, (dec_matrix, proc_matrix, far_into, far_from)
    )
    far_shape = far_src.shape + (w_mix.shape[0],)
    mesh_scale = norm_scale(gathered)
    latent_f = gathered * mesh_scale
    mesh_latent = latent_f.astype(jnp.bfloat16)
    far_out = contract_rows(far_from, mesh_latent).astype(jnp.bfloat16)
    far_rows = send_far(far_out.reshape(far_shape)).reshape(-1, far_shape[-1])
    before = passed_along(mesh_latent[mesh_rows - HALO :], axes, 1)
    after = passed_along(mesh_latent[:HALO], axes, -1)
    extended = jnp.concatenate([before, mesh_latent, after], axis=0)
    proc_sum = times(proc_matrix, extended) + times(far_into, far_rows)
    mixed_in = mesh_latent.astype(jnp.float32) + proc_sum
    proc_scale = norm_scale(mixed_in)
    proc_norm = mixed_in * proc_scale
    normed = proc_norm.astype(jnp.bfloat16)
    pre_mix = jnp.dot(normed, w_mix, preferred_element_type=jnp.float32)
    hidden = jax.nn.silu(pre_mix).astype(jnp.bfloat16)
    processed = (
        mesh_latent.astype(jnp.float32)
        + jnp.dot(hidden, w_back, preferred_element_type=jnp.float32)
    ).astype(jnp.bfloat16)
    near_processed = pull_blocks(processed)
    decoded = contract_rows(dec_matrix, near_processed)
    grid_in = embedded.astype(jnp.float32) + decoded
    grid_scale = norm_scale(grid_in)
    grid_norm = grid_in * grid_scale
    grid_node_state = grid_norm.astype(jnp.bfloat16)
    predicted_fields = jnp.dot(
        grid_node_state, head_projection_weight, preferred_element_type=jnp.float32
    )
    residual_error = predicted_fields - targets.astype(jnp.float32)
    loss_part = 0.5 * jnp.sum(node_weight[:, None] * residual_error * residual_error)
    weighted_error = (node_weight[:, None] * residual_error).astype(jnp.bfloat16)
    d_state = times_transpose(weighted_error, head_projection_weight)
    d_grid = norm_back(d_state, grid_norm, grid_scale)
    dec_partial = times(dec_matrix, d_grid.astype(jnp.bfloat16)).astype(jnp.bfloat16)
    head_part = contract_rows(weighted_error, grid_node_state)
    d_processed, (head_part, loss_part) = push_blocks(
        dec_partial, mesh_rows, (head_part, loss_part)
    )
    processed_grad = d_processed.astype(jnp.bfloat16)
    d_pre_mix = (times_transpose(processed_grad, w_back) * silu_slope(pre_mix)).astype(jnp.bfloat16)
    d_normed = times_transpose(d_pre_mix, w_mix)
    d_proc = norm_back(d_normed, proc_norm, proc_scale)
    d_proc_b = d_proc.astype(jnp.bfloat16)
    far_back = send_far(times(far_into.T, d_proc_b).astype(jnp.bfloat16).reshape(far_shape))
    far_spread = times(far_from, far_back.reshape(-1, far_shape[-1]))
    spread = contract_rows(proc_matrix, d_proc_b)
    rims = spread.astype(jnp.bfloat16)
    from_left = passed_along(rims[mesh_rows + HALO :], axes, 1).astype(jnp.float32)
    from_right = passed_along(rims[:HALO], axes, -1).astype(jnp.float32)
    from_left = jnp.pad(from_left, ((0, mesh_rows - HALO), (0, 0)))
    from_right = jnp.pad(from_right, ((mesh_rows - HALO, 0), (0, 0)))
    inner_part = spread[HALO : HALO + mesh_rows]
    width = w_mix.shape[0]
    early_part = jnp.concatenate(
        [
            contract_rows(normed, d_pre_mix),
            contract_rows(hidden, processed_grad),
            head_part,
            jnp.broadcast_to(loss_part, (1, width)),
        ],
        axis=0,
    )
    early_total = lax.psum(early_part, axes)
    d_latent = d_processed + d_proc + inner_part + from_left + from_right + far_spread
    d_gathered = norm_back(d_latent, latent_f, mesh_scale)
    enc_back = d_gathered.astype(jnp.bfloat16)
    near_back = pull_blocks(enc_back)
    d_embedded = d_grid + contract_rows(enc_matrix, near_back)
    d_pre_embed = (d_embedded * silu_slope(pre_embed)).astype(jnp.bfloat16)
    input_gradient = times_transpose(d_pre_embed, w_embed).astype(jnp.bfloat16)
    embed_total = added_up(contract_rows(inputs, d_pre_embed), axes)
    return (
        predicted_fields.astype(jnp.bfloat16),
        input_gradient,
        embed_total / total_grid,
        early_total[:width] / total_grid,
        early_total[width : 2 * width] / total_grid,
        early_total[2 * width : -1].T / total_grid,
        early_total[-1, :1] / total_grid,
    )


def solution(mesh):
    placed = (
        P(("groups", "mesh", "sub"), None),
        P(("groups", "mesh", "sub"), None),
        P(("mesh", "sub")),
        P(),
        P(),
        P(),
        P(),
        P(("mesh", "sub"), None, None),
        P(("mesh", "sub"), None, None),
        P(("mesh", "sub"), None, None),
        P(("mesh", "sub"), None),
        P(("mesh", "sub"), None),
        P(("mesh", "sub"), None),
        P(("mesh", "sub"), None),
        P(("mesh", "sub")),
        P(("mesh", "sub"), None),
        P(("mesh", "sub"), None),
        P(("mesh", "sub"), None),
        P(("mesh", "sub")),
        P(("mesh", "sub"), None, None),
        P(("mesh", "sub"), None, None),
        P(("mesh", "sub"), None, None),
        P(("mesh", "sub"), None),
    )
    return jax.shard_map(
        per_device,
        mesh=mesh,
        in_specs=placed,
        out_specs=(
            P(("groups", "mesh", "sub"), None),
            P(("groups", "mesh", "sub"), None),
            P("groups", None),
            P("groups", None),
            P("groups", None),
            P("groups", None),
            P("groups"),
        ),
        check_vma=False,
    )
```

time: 933 us -> 282 us (0.30)
  other arithmetic: 414 us -> 11.2 us
  waiting for transfers between devices: 224 us -> 112 us
  starting transfers between devices: 122 us -> 53.8 us
  local copies, waits for them, and re-layouts: 87.1 us -> 18.9 us
  matrix products: 26.8 us -> 67 us
  blocking collectives: 31.1 us -> 0 us
    scatter-add x16 -> x0, other arithmetic: 373 us -> none  [the longest x12 251 us: sum_rows(): jax.ops.segment_sum(values.reshape(-1, columns).astype(jnp.float32), segm...]
    ppermute x24 -> x20, waiting for transfers between devices: 152 us -> 51.8 us  [passed_along(): return lax.ppermute(block, axis, route)]
    gather x6 -> x0, local copies, waits for them, and re-layouts: 68.9 us -> none  [the longest x1 45.5 us: per_device(): d_grid[dec_dst[0]]]
    ppermute x24 -> x20, starting transfers between devices: 106 us -> 37.3 us  [passed_along(): return lax.ppermute(block, axis, route)]
    dot_general x0 -> x9, matrix products: none -> 34 us  [the longest x3 23.8 us: edge_matrix(): lax.dot_general(left, right, (((last,), (last,)), (batch, batch)), prefer...]
    psum x1 -> x0, blocking collectives: 31.1 us -> none  [per_device(): lax.psum((contract_rows(inputs, d_pre_embed), contract_rows(normed, d_pre...]
    psum x1, waiting for transfers between devices: 67.1 us -> 46.6 us  [per_device(): early_total = lax.psum(early_part, axes)]
    convert_element_type x4 -> x2, other arithmetic: 17.6 us -> 0.05 us  [one_hot(): return jnp.where(hit, marks, 0.0).astype(jnp.bfloat16)]
  transfers between devices with their start and end apart: 31 -> 25, of which waited for: 12 -> 10; matrix products, arithmetic and copies ran while one was open for 15% -> 19% of each run, Pallas kernels for 0% -> 0%
where the time goes in v1:
time: 282 us; the launch traced here: 281 us
  waiting for transfers between devices  112 us (40%)
  matrix products  67 us (24%)
  starting transfers between devices  53.8 us (19%)
  local copies, waits for them, and re-layouts  18.9 us (7%)
  between operations  18.1 us (6%)
  other arithmetic  11.2 us (4%)
    ppermute x20, waiting for transfers between devices, passed_along(): return lax.ppermute(block, axis, route)  51.8 us
    psum x1, waiting for transfers between devices, per_device(): early_total = lax.psum(early_part, axes)  46.6 us
    ppermute x20, starting transfers between devices, passed_along(): return lax.ppermute(block, axis, route)  37.3 us
    dot_general x8, matrix products, contract_rows(): lax.dot_general(left, right, (((0,), (0,)), ((), ())), preferred_element_...  24.3 us
    dot_general x3, matrix products, edge_matrix(): lax.dot_general(left, right, (((last,), (last,)), (batch, batch)), prefer...  23.8 us
    all_to_all x4, starting transfers between devices, send_far(): lax.all_to_all(values, ('mesh', 'sub'), split_axis=0, concat_axis=0, tile...  16.5 us
    all_to_all x4, waiting for transfers between devices, send_far(): lax.all_to_all(values, ('mesh', 'sub'), split_axis=0, concat_axis=0, tile...  14.1 us
    dot_general x6, matrix products, times(): return jnp.dot(left, right, preferred_element_type=jnp.float32)  10.2 us
  transfers between devices with their start and end apart: 25, of which 10 were waited for; matrix products, arithmetic and copies ran while one was open for 19% of the time, Pallas kernels for 0%

profile of v1, /device:TPU:0, one launch (start us, length us, event | category | flops | bytes accessed | tf_op | source)
XLA Modules:
  0.0 281.5 jit_solution(7777504441644275527)
XLA Ops:
  10.6 7.2 %fusion.11 = bf16[5,320,2048]{2,1,0:T(8,128)(2,1)S(1)} fusion(s32[5,1024]{1,0:T(8,128)S(1)} %get-tuple-element.73, bf16[5,1024]{1,0:T(8,128)(2,1)S(1)} %bitcast_select_fusion.1, s32[5,1024]{1,0:T(8,128)S(1)} %get-tuple-element.74), kind=kOutput, calls=%fused_computation.19 | convolution fusion | flops 6748897280 | bytes 6604800 | tf_op jit(solution)/shard_map/dot_general | solution.py:50
  17.9 3.8 %convolution_convert_fusion.1 = bf16[1600,512]{1,0:T(8,128)(2,1)S(1)} fusion(bf16[1600,2048]{1,0:T(8,128)(2,1)S(1)} %bitcast.59, f32[2048,512]{0,1:T(8,128)S(1)} %fusion.65), kind=kOutput, calls=%fused_computation.35 | convolution fusion | flops 3361505280 | bytes 12386304 | tf_op jit(solution)/shard_map/dot_general | solution.py:103
  25.5 4.4 %collective-permute-start.1 = (bf16[320,512]{1,0:T(8,128)(2,1)S(1)}, bf16[320,512]{1,0:T(8,128)(2,1)}, u32[]{:S(2)}, u32[]{:S(2)}) collective-permute-start(bf16[320,512]{1,0:T(8,128)(2,1)S(1)} %get-tuple-element.56), channel_id=1, source_target_pairs={{1,0},{2,1},{3,2},{4,3},{5,4},{6,5},{7,6},{8,7},{9,8},{10,9},{11,1... | collective-permute-start | bytes 983048 | tf_op jit(solution)/shard_map/ppermute | solution.py:17
  31.9 15.6 %fusion.12 = bf16[5,320,2048]{2,1,0:T(8,128)(2,1)} fusion(s32[5,2048]{1,0:T(8,128)S(1)} %get-tuple-element.75, bf16[5,2048]{1,0:T(8,128)(2,1)S(1)} %bitcast_select_fusion, s32[5,2048]{1,0:T(8,128)S(1)} %get-tuple-element.76), kind=kOutput, calls=%fused_computation.20 | convolution fusion | flops 13494517760 | bytes 6656000 | tf_op jit(solution)/shard_map/dot_general | solution.py:50
  53.2 3.5 %all-to-all-start = ((bf16[16,4,512]{2,1,0:T(4,128)(2,1)}), bf16[16,4,512]{2,1,0:T(4,128)(2,1)S(1)}, u32[]{:S(2)}, u32[]{:S(2)}) async-start(bf16[16,4,512]{2,1,0:T(4,128)(2,1)} %reshape.144), calls=%async_computation | async-start | bytes 131072 | tf_op jit(solution)/shard_map/all_to_all | solution.py:82
  57.1 4.2 %collective-permute-start.5 = (bf16[32,512]{1,0:T(8,128)(2,1)S(1)}, bf16[32,512]{1,0:T(8,128)(2,1)S(1)}, u32[]{:S(2)}, u32[]{:S(2)}) collective-permute-start(bf16[32,512]{1,0:T(8,128)(2,1)S(1)} %get-tuple-element.61), channel_id=1, source_target_pairs={{1,0},{2,1},{3,2},{4,3},{5,4},{6,5},{7,6},{8,7},{9,8},{10,9},{11,1... | collective-permute-start | bytes 98312 | tf_op jit(solution)/shard_map/ppermute | solution.py:17
  65.6 4.6 %collective-permute-start.9 = (bf16[320,512]{1,0:T(8,128)(2,1)S(1)}, bf16[320,512]{1,0:T(8,128)(2,1)S(1)}, u32[]{:S(2)}, u32[]{:S(2)}) collective-permute-start(bf16[320,512]{1,0:T(8,128)(2,1)S(1)} %fusion.26), channel_id=1, source_target_pairs={{2,0},{3,1},{4,2},{5,3},{6,4},{7,5},{8,6},{9,7},{10,8},{11,9},{12,... | collective-permute-start | bytes 983048 | tf_op jit(solution)/shard_map/ppermute | solution.py:17
  71.7 12.4 %collective-permute-done.6 = bf16[320,512]{1,0:T(8,128)(2,1)S(1)} collective-permute-done((bf16[320,512]{1,0:T(8,128)(2,1)S(1)}, bf16[320,512]{1,0:T(8,128)(2,1)S(1)}, u32[]{:S(2)}, u32[]{:S(2)}) %collective-permute-start.6) | collective-permute-done | bytes 327712 | tf_op jit(solution)/shard_map/ppermute | solution.py:17
  86.6 5.2 %multiply_reduce_fusion.1 = (f32[2048]{0:T(1024)S(1)}, f32[2048,512]{0,1:T(8,128)S(1)}) fusion(bf16[1600,2048]{1,0:T(8,128)(2,1)S(1)} %bitcast.61, bf16[1600,512]{1,0:T(8,128)(2,1)S(1)} %constant_dynamic-update-slice_fusion, f32[2048,512]{0,1:T(8,128)S(1)} %copy-done.3), kind=kOutput, calls=%fused_computation.24 | convolution fusion | flops 3364878336 | bytes 16588800 | tf_op jit(solution)/shard_map/dot_general | solution.py:97
  96.2 3.8 %convolution_convert_fusion = bf16[1600,512]{1,0:T(8,128)(2,1)S(1)} fusion(bf16[1600,2048]{1,0:T(8,128)(2,1)S(1)} %bitcast.62, f32[2048,512]{0,1:T(8,128)S(1)} %get-tuple-element.68, f32[2048,512]{0,1:T(8,128)S(1)} %get-tuple-element.65, f32[2048]{0:T(1024)S(1)} %broadcast_multiply_fusion, f32[2048]{0:T(1024)S(1)} %add_rsqrt_fusion), kind=kOutput, calls=%fused_computation.34 | convolution fusion | flops 3361505280 | bytes 16596992 | tf_op jit(solution)/shard_map/dot_general | solution.py:103
  104.8 4.2 %collective-permute-start.11 = (bf16[320,512]{1,0:T(8,128)(2,1)}, bf16[320,512]{1,0:T(8,128)(2,1)}, u32[]{:S(2)}, u32[]{:S(2)}) collective-permute-start(bf16[320,512]{1,0:T(8,128)(2,1)} %get-tuple-element.51), channel_id=1, source_target_pairs={{1,0},{2,1},{3,2},{4,3},{5,4},{6,5},{7,6},{8,7},{9,8},{10,9},{11,1... | collective-permute-start | bytes 983048 | tf_op jit(solution)/shard_map/ppermute | solution.py:17
  109.9 3.8 %fusion.30 = f32[227,512]{1,0:T(8,128)} fusion(bf16[2048,227]{0,1:T(8,128)(2,1)S(1)} %get-tuple-element.44, f32[2048,512]{0,1:T(8,128)} %copy-done.1, f32[2048]{0:T(1024)S(1)} %add_rsqrt_fusion), kind=kOutput, calls=%fused_computation.64 | convolution fusion | flops 478150656 | bytes 5597184 | tf_op jit(solution)/shard_map/dot_general | solution.py:97
  113.7 9.7 %collective-permute-done.13 = bf16[320,512]{1,0:T(8,128)(2,1)} collective-permute-done((bf16[320,512]{1,0:T(8,128)(2,1)}, bf16[320,512]{1,0:T(8,128)(2,1)}, u32[]{:S(2)}, u32[]{:S(2)}) %collective-permute-start.13) | collective-permute-done | bytes 327712 | tf_op jit(solution)/shard_map/ppermute | solution.py:17
  123.3 5.4 %collective-permute-done.10 = bf16[320,512]{1,0:T(8,128)(2,1)} collective-permute-done((bf16[320,512]{1,0:T(8,128)(2,1)}, bf16[320,512]{1,0:T(8,128)(2,1)}, u32[]{:S(2)}, u32[]{:S(2)}) %collective-permute-start.10) | collective-permute-done | bytes 327712 | tf_op jit(solution)/shard_map/ppermute | solution.py:17
  134.4 3.5 %all-to-all-start.1 = ((bf16[16,4,512]{2,1,0:T(4,128)(2,1)}), bf16[16,4,512]{2,1,0:T(4,128)(2,1)S(1)}, u32[]{:S(2)}, u32[]{:S(2)}) async-start(bf16[16,4,512]{2,1,0:T(4,128)(2,1)} %reshape.146), calls=%async_computation.1 | async-start | bytes 131072 | tf_op jit(solution)/shard_map/all_to_all | solution.py:82
  138.9 4.2 %collective-permute-start.15 = (bf16[32,512]{1,0:T(8,128)(2,1)}, bf16[32,512]{1,0:T(8,128)(2,1)S(1)}, u32[]{:S(2)}, u32[]{:S(2)}) collective-permute-start(bf16[32,512]{1,0:T(8,128)(2,1)} %get-tuple-element.59), channel_id=1, source_target_pairs={{1,0},{2,1},{3,2},{4,3},{5,4},{6,5},{7,6},{8,7},{9,8},{10,9},{11,1... | collective-permute-start | bytes 98312 | tf_op jit(solution)/shard_map/ppermute | solution.py:17
  150.8 8.1 %concatenate.15 = f32[1252,512]{1,0:T(8,128)} concatenate(f32[512,512]{1,0:T(8,128)S(1)} %fusion.57, f32[512,512]{1,0:T(8,128)} %fusion.44, f32[227,512]{1,0:T(8,128)} %fusion.30, f32[1,512]{1,0:T(1,128)S(1)} %broadcast_in_dim.139), dimensions={0} | concatenate | bytes 5128192 | tf_op jit(solution)/shard_map/concatenate | solution.py:215
  158.9 3.8 %collective-permute-start.19 = (bf16[320,512]{1,0:T(8,128)(2,1)}, bf16[320,512]{1,0:T(8,128)(2,1)S(1)}, u32[]{:S(2)}, u32[]{:S(2)}) collective-permute-start(bf16[320,512]{1,0:T(8,128)(2,1)} %multiply_convert_fusion.6), channel_id=1, source_target_pairs={{2,0},{3,1},{4,2},{5,3},{6,4},{7,5},{8,6},{9,7},{10,8},{11,9},{12,... | collective-permute-start | bytes 983048 | tf_op jit(solution)/shard_map/ppermute | solution.py:17
  165.3 20.1 %collective-permute-done.18 = bf16[320,512]{1,0:T(8,128)(2,1)S(1)} collective-permute-done((bf16[320,512]{1,0:T(8,128)(2,1)}, bf16[320,512]{1,0:T(8,128)(2,1)S(1)}, u32[]{:S(2)}, u32[]{:S(2)}) %collective-permute-start.18) | collective-permute-done | bytes 327712 | tf_op jit(solution)/shard_map/ppermute | solution.py:17
  185.5 11.1 %multiply_convert_fusion = bf16[2048,512]{0,1:T(8,128)(2,1)S(1)} fusion(f32[2048,512]{0,1:T(8,128)} %copy-done.2, bf16[1600,2048]{1,0:T(8,128)(2,1)} %bitcast.60, bf16[1600,512]{1,0:T(8,128)(2,1)S(1)} %constant_dynamic-update-slice_fusion.5, f32[2048,512]{0,1:T(8,128)} %copy-done.4, f32[2048]{0:T(1024)S(1)} %copy-done.31, f32[2048,512]{0,1:T(8,128)} %copy-done.1, ...), kind=kOutput, calls=%fused_computation.21 | convolution fusion | flops 3370123264 | bytes 22888448 | tf_op jit(solution)/shard_map/dot_general | solution.py:97
  198.0 5.9 %all-to-all-start.2 = ((bf16[16,16,512]{2,1,0:T(8,128)(2,1)}), bf16[16,16,512]{2,1,0:T(8,128)(2,1)S(1)}, u32[]{:S(2)}, u32[]{:S(2)}) async-start(bf16[16,16,512]{2,1,0:T(8,128)(2,1)} %bitcast.6), calls=%async_computation.2 | async-start | bytes 524288 | tf_op jit(solution)/shard_map/all_to_all | solution.py:82
  205.5 9.4 %all-to-all-done.2 = bf16[16,16,512]{2,1,0:T(8,128)(2,1)S(1)} async-done(((bf16[16,16,512]{2,1,0:T(8,128)(2,1)}), bf16[16,16,512]{2,1,0:T(8,128)(2,1)S(1)}, u32[]{:S(2)}, u32[]{:S(2)}) %all-to-all-start.2) | async-done | bytes 262176 | tf_op jit(solution)/shard_map/all_to_all | solution.py:82
  215.7 3.7 %all-to-all-start.3 = ((bf16[16,16,512]{2,1,0:T(8,128)(2,1)}), bf16[16,16,512]{2,1,0:T(8,128)(2,1)S(1)}, u32[]{:S(2)}, u32[]{:S(2)}) async-start(bf16[16,16,512]{2,1,0:T(8,128)(2,1)} %broadcast_in_dim.138), calls=%async_computation.3 | async-start | bytes 524288 | tf_op jit(solution)/shard_map/all_to_all | solution.py:82
  219.3 46.6 %all-reduce.5.cloned.1.call-done = f32[1252,512]{1,0:T(8,128)} async-done(((f32[1252,512]{1,0:T(8,128)}), f32[1252,512]{1,0:T(8,128)}) %all-reduce.5.cloned.1.call-update) | async-done | bytes 2564112 | tf_op jit(solution)/shard_map/psum | solution.py:224
  (188 shorter events, 59.3 us)
Async XLA Ops:
  22.6 26.0 %collective-permute-start.3 = (bf16[320,512]{1,0:T(8,128)(2,1)}, bf16[320,512]{1,0:T(8,128)(2,1)}, u32[]{:S(2)}, u32[]{:S(2)}) collective-permute-start(bf16[320,512]{1,0:T(8,128)(2,1)} %get-tuple-element.53), channel_id=1, source_target_pairs={{14,0},{15,1},{0,2},{1,3},{2,4},{3,5},{4,6},{5,7},{6,8},{7,9},{8,1... | collective-permute-start | bytes 983048 | tf_op jit(solution)/shard_map/ppermute | solution.py:17
  25.5 23.1 %collective-permute-start.2 = (bf16[320,512]{1,0:T(8,128)(2,1)S(1)}, bf16[320,512]{1,0:T(8,128)(2,1)}, u32[]{:S(2)}, u32[]{:S(2)}) collective-permute-start(bf16[320,512]{1,0:T(8,128)(2,1)S(1)} %get-tuple-element.54), channel_id=1, source_target_pairs={{15,0},{0,1},{1,2},{2,3},{3,4},{4,5},{5,6},{6,7},{7,8},{8,9},{9,10... | collective-permute-start | bytes 983048 | tf_op jit(solution)/shard_map/ppermute | solution.py:17
  25.5 23.1 %collective-permute-start.1 = (bf16[320,512]{1,0:T(8,128)(2,1)S(1)}, bf16[320,512]{1,0:T(8,128)(2,1)}, u32[]{:S(2)}, u32[]{:S(2)}) collective-permute-start(bf16[320,512]{1,0:T(8,128)(2,1)S(1)} %get-tuple-element.56), channel_id=1, source_target_pairs={{1,0},{2,1},{3,2},{4,3},{5,4},{6,5},{7,6},{8,7},{9,8},{10,9},{11,1... | collective-permute-start | bytes 983048 | tf_op jit(solution)/shard_map/ppermute | solution.py:17
  29.9 20.7 %collective-permute-start = (bf16[320,512]{1,0:T(8,128)(2,1)S(1)}, bf16[320,512]{1,0:T(8,128)(2,1)}, u32[]{:S(2)}, u32[]{:S(2)}) collective-permute-start(bf16[320,512]{1,0:T(8,128)(2,1)S(1)} %get-tuple-element.57), channel_id=1, source_target_pairs={{2,0},{3,1},{4,2},{5,3},{6,4},{7,5},{8,6},{9,7},{10,8},{11,9},{12,... | collective-permute-start | bytes 983048 | tf_op jit(solution)/shard_map/ppermute | solution.py:17
  53.2 10.7 %all-to-all-start = ((bf16[16,4,512]{2,1,0:T(4,128)(2,1)}), bf16[16,4,512]{2,1,0:T(4,128)(2,1)S(1)}, u32[]{:S(2)}, u32[]{:S(2)}) async-start(bf16[16,4,512]{2,1,0:T(4,128)(2,1)} %reshape.144), calls=%async_computation | async-start | bytes 131072 | tf_op jit(solution)/shard_map/all_to_all | solution.py:82
  56.7 7.4 %collective-permute-start.4 = (bf16[32,512]{1,0:T(8,128)(2,1)S(1)}, bf16[32,512]{1,0:T(8,128)(2,1)S(1)}, u32[]{:S(2)}, u32[]{:S(2)}) collective-permute-start(bf16[32,512]{1,0:T(8,128)(2,1)S(1)} %get-tuple-element.60), channel_id=1, source_target_pairs={{15,0},{0,1},{1,2},{2,3},{3,4},{4,5},{5,6},{6,7},{7,8},{8,9},{9,10... | collective-permute-start | bytes 98312 | tf_op jit(solution)/shard_map/ppermute | solution.py:17
  57.1 7.1 %collective-permute-start.5 = (bf16[32,512]{1,0:T(8,128)(2,1)S(1)}, bf16[32,512]{1,0:T(8,128)(2,1)S(1)}, u32[]{:S(2)}, u32[]{:S(2)}) collective-permute-start(bf16[32,512]{1,0:T(8,128)(2,1)S(1)} %get-tuple-element.61), channel_id=1, source_target_pairs={{1,0},{2,1},{3,2},{4,3},{5,4},{6,5},{7,6},{8,7},{9,8},{10,9},{11,1... | collective-permute-start | bytes 98312 | tf_op jit(solution)/shard_map/ppermute | solution.py:17
  65.5 18.7 %collective-permute-start.6 = (bf16[320,512]{1,0:T(8,128)(2,1)S(1)}, bf16[320,512]{1,0:T(8,128)(2,1)S(1)}, u32[]{:S(2)}, u32[]{:S(2)}) collective-permute-start(bf16[320,512]{1,0:T(8,128)(2,1)S(1)} %fusion.26), channel_id=1, source_target_pairs={{14,0},{15,1},{0,2},{1,3},{2,4},{3,5},{4,6},{5,7},{6,8},{7,9},{8,1... | collective-permute-start | bytes 983048 | tf_op jit(solution)/shard_map/ppermute | solution.py:17
  65.5 18.6 %collective-permute-start.7 = (bf16[320,512]{1,0:T(8,128)(2,1)S(1)}, bf16[320,512]{1,0:T(8,128)(2,1)S(1)}, u32[]{:S(2)}, u32[]{:S(2)}) collective-permute-start(bf16[320,512]{1,0:T(8,128)(2,1)S(1)} %fusion.26), channel_id=1, source_target_pairs={{15,0},{0,1},{1,2},{2,3},{3,4},{4,5},{5,6},{6,7},{7,8},{8,9},{9,10... | collective-permute-start | bytes 983048 | tf_op jit(solution)/shard_map/ppermute | solution.py:17
  65.6 20.9 %collective-permute-start.9 = (bf16[320,512]{1,0:T(8,128)(2,1)S(1)}, bf16[320,512]{1,0:T(8,128)(2,1)S(1)}, u32[]{:S(2)}, u32[]{:S(2)}) collective-permute-start(bf16[320,512]{1,0:T(8,128)(2,1)S(1)} %fusion.26), channel_id=1, source_target_pairs={{2,0},{3,1},{4,2},{5,3},{6,4},{7,5},{8,6},{9,7},{10,8},{11,9},{12,... | collective-permute-start | bytes 983048 | tf_op jit(solution)/shard_map/ppermute | solution.py:17
  70.3 14.0 %collective-permute-start.8 = (bf16[320,512]{1,0:T(8,128)(2,1)S(1)}, bf16[320,512]{1,0:T(8,128)(2,1)S(1)}, u32[]{:S(2)}, u32[]{:S(2)}) collective-permute-start(bf16[320,512]{1,0:T(8,128)(2,1)S(1)} %fusion.26), channel_id=1, source_target_pairs={{1,0},{2,1},{3,2},{4,3},{5,4},{6,5},{7,6},{8,7},{9,8},{10,9},{11,1... | collective-permute-start | bytes 983048 | tf_op jit(solution)/shard_map/ppermute | solution.py:17
  101.1 22.2 %collective-permute-start.13 = (bf16[320,512]{1,0:T(8,128)(2,1)}, bf16[320,512]{1,0:T(8,128)(2,1)}, u32[]{:S(2)}, u32[]{:S(2)}) collective-permute-start(bf16[320,512]{1,0:T(8,128)(2,1)} %get-tuple-element.48), channel_id=1, source_target_pairs={{14,0},{15,1},{0,2},{1,3},{2,4},{3,5},{4,6},{5,7},{6,8},{7,9},{8,1... | collective-permute-start | bytes 983048 | tf_op jit(solution)/shard_map/ppermute | solution.py:17
  104.5 18.9 %collective-permute-start.12 = (bf16[320,512]{1,0:T(8,128)(2,1)}, bf16[320,512]{1,0:T(8,128)(2,1)}, u32[]{:S(2)}, u32[]{:S(2)}) collective-permute-start(bf16[320,512]{1,0:T(8,128)(2,1)} %get-tuple-element.49), channel_id=1, source_target_pairs={{15,0},{0,1},{1,2},{2,3},{3,4},{4,5},{5,6},{6,7},{7,8},{8,9},{9,10... | collective-permute-start | bytes 983048 | tf_op jit(solution)/shard_map/ppermute | solution.py:17
  104.8 18.6 %collective-permute-start.11 = (bf16[320,512]{1,0:T(8,128)(2,1)}, bf16[320,512]{1,0:T(8,128)(2,1)}, u32[]{:S(2)}, u32[]{:S(2)}) collective-permute-start(bf16[320,512]{1,0:T(8,128)(2,1)} %get-tuple-element.51), channel_id=1, source_target_pairs={{1,0},{2,1},{3,2},{4,3},{5,4},{6,5},{7,6},{8,7},{9,8},{10,9},{11,1... | collective-permute-start | bytes 983048 | tf_op jit(solution)/shard_map/ppermute | solution.py:17
  108.9 19.8 %collective-permute-start.10 = (bf16[320,512]{1,0:T(8,128)(2,1)}, bf16[320,512]{1,0:T(8,128)(2,1)}, u32[]{:S(2)}, u32[]{:S(2)}) collective-permute-start(bf16[320,512]{1,0:T(8,128)(2,1)} %get-tuple-element.52), channel_id=1, source_target_pairs={{2,0},{3,1},{4,2},{5,3},{6,4},{7,5},{8,6},{9,7},{10,8},{11,9},{12,... | collective-permute-start | bytes 983048 | tf_op jit(solution)/shard_map/ppermute | solution.py:17
  134.4 10.7 %all-to-all-start.1 = ((bf16[16,4,512]{2,1,0:T(4,128)(2,1)}), bf16[16,4,512]{2,1,0:T(4,128)(2,1)S(1)}, u32[]{:S(2)}, u32[]{:S(2)}) async-start(bf16[16,4,512]{2,1,0:T(4,128)(2,1)} %reshape.146), calls=%async_computation.1 | async-start | bytes 131072 | tf_op jit(solution)/shard_map/all_to_all | solution.py:82
  137.9 128.0 %all-reduce.5.cloned.1.call-start = ((), (), s32[]{:S(2)}) async-start(), calls=%async_computation.4 | async-start | bytes 5144576 | tf_op jit(solution)/shard_map/psum | solution.py:224
  138.6 6.5 %collective-permute-start.14 = (bf16[32,512]{1,0:T(8,128)(2,1)}, bf16[32,512]{1,0:T(8,128)(2,1)S(1)}, u32[]{:S(2)}, u32[]{:S(2)}) collective-permute-start(bf16[32,512]{1,0:T(8,128)(2,1)} %get-tuple-element.58), channel_id=1, source_target_pairs={{15,0},{0,1},{1,2},{2,3},{3,4},{4,5},{5,6},{6,7},{7,8},{8,9},{9,10... | collective-permute-start | bytes 98312 | tf_op jit(solution)/shard_map/ppermute | solution.py:17
  147.8 16.4 %collective-permute-start.16 = (bf16[320,512]{1,0:T(8,128)(2,1)}, bf16[320,512]{1,0:T(8,128)(2,1)S(1)}, u32[]{:S(2)}, u32[]{:S(2)}) collective-permute-start(bf16[320,512]{1,0:T(8,128)(2,1)} %multiply_convert_fusion.6), channel_id=1, source_target_pairs={{14,0},{15,1},{0,2},{1,3},{2,4},{3,5},{4,6},{5,7},{6,8},{7,9},{8,1... | collective-permute-start | bytes 983048 | tf_op jit(solution)/shard_map/ppermute | solution.py:17
  149.3 15.0 %collective-permute-start.17 = (bf16[320,512]{1,0:T(8,128)(2,1)}, bf16[320,512]{1,0:T(8,128)(2,1)S(1)}, u32[]{:S(2)}, u32[]{:S(2)}) collective-permute-start(bf16[320,512]{1,0:T(8,128)(2,1)} %multiply_convert_fusion.6), channel_id=1, source_target_pairs={{15,0},{0,1},{1,2},{2,3},{3,4},{4,5},{5,6},{6,7},{7,8},{8,9},{9,10... | collective-permute-start | bytes 983048 | tf_op jit(solution)/shard_map/ppermute | solution.py:17
  158.9 26.5 %collective-permute-start.19 = (bf16[320,512]{1,0:T(8,128)(2,1)}, bf16[320,512]{1,0:T(8,128)(2,1)S(1)}, u32[]{:S(2)}, u32[]{:S(2)}) collective-permute-start(bf16[320,512]{1,0:T(8,128)(2,1)} %multiply_convert_fusion.6), channel_id=1, source_target_pairs={{2,0},{3,1},{4,2},{5,3},{6,4},{7,5},{8,6},{9,7},{10,8},{11,9},{12,... | collective-permute-start | bytes 983048 | tf_op jit(solution)/shard_map/ppermute | solution.py:17
  162.8 22.6 %collective-permute-start.18 = (bf16[320,512]{1,0:T(8,128)(2,1)}, bf16[320,512]{1,0:T(8,128)(2,1)S(1)}, u32[]{:S(2)}, u32[]{:S(2)}) collective-permute-start(bf16[320,512]{1,0:T(8,128)(2,1)} %multiply_convert_fusion.6), channel_id=1, source_target_pairs={{1,0},{2,1},{3,2},{4,3},{5,4},{6,5},{7,6},{8,7},{9,8},{10,9},{11,1... | collective-permute-start | bytes 983048 | tf_op jit(solution)/shard_map/ppermute | solution.py:17
  198.0 16.8 %all-to-all-start.2 = ((bf16[16,16,512]{2,1,0:T(8,128)(2,1)}), bf16[16,16,512]{2,1,0:T(8,128)(2,1)S(1)}, u32[]{:S(2)}, u32[]{:S(2)}) async-start(bf16[16,16,512]{2,1,0:T(8,128)(2,1)} %bitcast.6), calls=%async_computation.2 | async-start | bytes 524288 | tf_op jit(solution)/shard_map/all_to_all | solution.py:82
  215.7 57.0 %all-to-all-start.3 = ((bf16[16,16,512]{2,1,0:T(8,128)(2,1)}), bf16[16,16,512]{2,1,0:T(8,128)(2,1)S(1)}, u32[]{:S(2)}, u32[]{:S(2)}) async-start(bf16[16,16,512]{2,1,0:T(8,128)(2,1)} %broadcast_in_dim.138), calls=%async_computation.3 | async-start | bytes 524288 | tf_op jit(solution)/shard_map/all_to_all | solution.py:82
  (42 other events, 472.3 us)
Sparse Core Ops, SparseCore 0:
  159.1 106.7 all-reduce.4
